TPU v7x, 512 devices: a whole 4x8x8 slice. The times are simulated.
512 devices in a mesh: gx: 16 (over z, core), gy: 32 (over x, y).
Axes of the slice: x: 4, y: 8, z: 8, core: 2. Of those that a mesh axis runs over, the one named last changes fastest.
Arguments:
- right_sides: float32 [64, 524288], P(None, ('gx', 'gy')), may hold values from -6 to 6
- points: float32 [3, 524288], P(None, ('gx', 'gy'))
- leaf_basis: bfloat16 [64, 524288], P(None, ('gx', 'gy')), may hold values from -0.75 to 0.75
- leaf_transfer: bfloat16 [64, 524288], P(None, ('gx', 'gy')), may hold values from -0.75 to 0.75
- upper_transfer: float32 [7, 2, 64, 64], replicated, may hold values from -0.5 to 0.5
- coupling: float32 [8, 3, 64, 64], replicated, may hold values from -0.109375 to 0.109375
- near_leaves: int32 [8192, 12], P(('gx', 'gy')), may hold values from 0 to 8191, as said below
- admissible: int32 [1020, 3], replicated, may hold values 0 or 1
Outputs:
- product: float32 [64, 524288], P(None, ('gx', 'gy'))
Inputs may be any that keep to these rules, and one draw needn't show every extreme that they name: `near_leaves`: each row lists 12 different leaves, all owned by the four devices whose gx index and gy index equal those of the row's own device but for the lowest bit.
All inputs are finite; a program needn't handle non-finite values.
Results may differ from a plain program's by a relative error of at most 0.0037.
Values sent between devices are 32-bit elements; how exact they have to be, the bound alone decides.
No kernel may reach another device: no remote copies, remote signals or barrier semaphores. Data moves between devices by JAX's collectives and lax.ppermute only.
A program may use at most 128 MiB of HBM per device.

v0:
```python
import jax
import jax.numpy as jnp
from jax import lax
from jax.experimental import pallas as pl
from jax.experimental.pallas import tpu as pltpu
from jax.sharding import PartitionSpec as P

ROOT_THREE = 1.7320508075688772
LENGTH_SCALE = 0.6
AMPLITUDE = 0.25
NUGGET = 0.5
LOG2_E = 1.4426950408889634
BITS_X = 4
BITS_Y = 5
DEVICES = 512
LEVELS = 9
LEAVES = 16
LEAF = 64
RANK = 64
HALF = 64
LANES = 128
F32 = jnp.float32
BF16 = jnp.bfloat16
NT = (((1,), (1,)), ((), ()))
VMEM = pl.BlockSpec(memory_space=pltpu.VMEM)
ANYWHERE = pl.BlockSpec(memory_space=pl.ANY)
SMEM = pl.BlockSpec(memory_space=pltpu.SMEM)


def places():
    listed = []
    for bit in range(max(BITS_X, BITS_Y)):
        if bit < BITS_X:
            listed.append(("x", bit))
        if bit < BITS_Y:
            listed.append(("y", bit))
    return listed


PLACES = places()
SOURCE = (2, 4, 6)
TARGET = (1, 3, 5, 7, 8)
GROUP_X = [z * 2 + core for z in (7, 3, 6, 2, 5, 1, 4, 0) for core in (1, 0)]
GROUP_Y = [x * 8 + y for y in (3, 7, 1, 5, 2, 6, 4, 0) for x in (1, 3, 2, 0)]

CLIMB, DOWN, FAR = {}, {}, {}
for _h in range(1, LEVELS - 2):
    for _side in range(2 if _h in SOURCE else 1):
        CLIMB[_h, _side] = len(CLIMB)
for _h in range(LEVELS - 2):
    for _side in range(2 if _h in TARGET else 1):
        DOWN[_h, _side] = len(CLIMB) + len(DOWN)
for _h in range(LEVELS - 1):
    for _step in (1, 2, 3):
        FAR[_h, _step] = len(CLIMB) + len(DOWN) + len(FAR)
WEIGHTS = len(CLIMB) + len(DOWN) + len(FAR)


def above(chosen, h):
    return [place for place in chosen if place >= h]


def flipped(chosen, h, step):
    listed = above(chosen, h)
    return sum(1 << listed.index(h + p) for p in (0, 1) if step >> p & 1 and h + p in listed)


def low_lanes(rows):
    return lax.broadcasted_iota(jnp.int32, (rows, LANES), 1) < HALF


def split_lanes(value):
    high = value.astype(BF16).astype(F32)
    return jnp.where(low_lanes(value.shape[0]), high, value - high).astype(BF16)


def split_rows(wide):
    high = wide.astype(BF16)
    return jnp.concatenate([high, (wide - high.astype(F32)).astype(BF16)], axis=0)


def block_diagonal(basis):
    wide = basis.astype(F32)
    leaf = lax.broadcasted_iota(jnp.int32, wide.shape, 1) // LEAF
    return jnp.concatenate([jnp.where(leaf == l, wide, 0.0).astype(BF16) for l in range(4)], axis=0)


def up_kernel(
    right_ref,
    points_ref,
    basis_ref,
    transfer_ref,
    upper_ref,
    lifted_ref,
    send_ref,
    points_in,
    basis_in,
    transfer_in,
    upper_in,
    sems,
):
    copies = [
        pltpu.make_async_copy(right_ref, send_ref.at[pl.ds(0, 64)], sems.at[0]),
        pltpu.make_async_copy(basis_ref, basis_in, sems.at[1]),
        pltpu.make_async_copy(transfer_ref, transfer_in, sems.at[2]),
        pltpu.make_async_copy(points_ref, points_in, sems.at[3]),
        pltpu.make_async_copy(upper_ref.at[0, lax.axis_index("gx") & 1], upper_in, sems.at[4]),
    ]
    for copy in copies:
        copy.start()
    for copy in copies:
        copy.wait()
    total = None
    for block in range(4):
        cols = slice(block * 256, block * 256 + 256)
        rounded = send_ref[:64, cols].astype(BF16)
        leaf_coeff = lax.dot_general(
            rounded, block_diagonal(basis_in[:, cols]), NT, preferred_element_type=F32
        ).astype(BF16)
        transfer = transfer_in[:, cols]
        part = lax.dot_general(
            leaf_coeff,
            jnp.concatenate([transfer, transfer], axis=0),
            NT,
            preferred_element_type=F32,
        )
        total = part if total is None else total + part
    matrix = upper_in[...]
    wide = split_rows(jnp.concatenate([matrix, matrix], axis=1))
    lifted = multiply([(split_lanes(total), wide)])
    halves = [fold(lifted[:32]), fold(lifted[32:])]
    for target in range(lifted_ref.shape[0]):
        lifted_ref[target] = halves[GROUP_X[target] % 2]
    send_ref[64:67, :] = points_in[...]
    packed = fold(total)
    for tile in range(8):
        cols = slice(tile * LANES, tile * LANES + LANES)
        send_ref[67:71, cols] = packed[tile * 4 : tile * 4 + 4]
    send_ref[71:72, :] = jnp.zeros((1, LEAVES * LEAF), F32)


def as_nodes(value):
    return [value[row : row + 32] for row in range(0, value.shape[0], 32)]


def device_index():
    index_x = lax.axis_index("gx")
    return index_x, lax.axis_index("gy"), index_x & 1


def device_sides():
    index_x, index_y, _ = device_index()
    return [(index_x if axis == "x" else index_y) >> bit & 1 for axis, bit in PLACES]


def place_index(sides, listed):
    index = jnp.int32(0)
    for bit, place in enumerate(listed):
        index = index + sides[place] * 2**bit
    return index


def sent_coeff(ref):
    return jnp.concatenate(
        [ref[67:71, tile * LANES : tile * LANES + LANES] for tile in range(8)], axis=0
    )


def fold(value):
    rows = value.shape[0] // 2
    return jnp.where(low_lanes(rows), value[:rows], value[rows:])


def unfold(packed):
    low = low_lanes(packed.shape[0])
    rolled = pltpu.roll(packed, HALF, 1)
    return jnp.concatenate(
        [jnp.where(low, packed, rolled), jnp.where(low, rolled, packed)], axis=0
    )


def multiply(pairs):
    left = [piece for value, _ in pairs for piece in (value, value)]
    right = [piece for _, m in pairs for piece in (m[:64], m[:64], m[64:], m[64:])]
    return jnp.dot(
        jnp.concatenate(left, axis=1),
        jnp.concatenate(right, axis=0),
        preferred_element_type=F32,
    )


def weights_kernel(upper_ref, coupling_ref, admissible_ref, out_ref):
    sides = device_sides()
    code = place_index(sides, range(LEVELS))

    def plain(matrix):
        return jnp.concatenate([matrix, matrix], axis=1)

    def transposed(matrix):
        return jnp.concatenate([matrix, matrix], axis=0).T

    for h in range(LEVELS - 2):
        for side in range(2):
            matrix = upper_ref[h, sides[h] ^ side]
            if (h, side) in CLIMB:
                out_ref[CLIMB[h, side]] = split_rows(plain(matrix))
            if (h, side) in DOWN:
                out_ref[DOWN[h, side]] = split_rows(transposed(matrix))
    for h in range(LEVELS - 1):
        first = 2 * DEVICES - 2 * DEVICES // 2**h
        for step in (1, 2, 3):
            turned = sum(1 << p for p in (0, 1) if step >> p & 1 and h + p in TARGET)
            target = (code >> h) ^ (turned if h else 0)
            here = target & 3
            there = here ^ step
            matrix = coupling_ref[h, jnp.abs(there - here) - 1]
            flag = admissible_ref[step - 1, first + target].astype(F32)
            upward = jnp.full((64, LANES), there - here, jnp.int32) > 0
            chosen = jnp.where(upward, transposed(matrix), plain(matrix))
            out_ref[FAR[h, step]] = split_rows(chosen * flag)


def tree_kernel(gathered_ref, weights_ref, out_ref, tie_ref, downs):
    sides = device_sides()
    own_source = place_index(sides, SOURCE)
    own_target = place_index(sides, TARGET)
    nodes = []
    for relative in range(2 ** len(SOURCE)):
        far_z = own_source ^ relative ^ 7
        first = (far_z & 3) * 4 + (far_z >> 2) * 2
        nodes.append(split_lanes(unfold(gathered_ref[first] + gathered_ref[first + 1])))
    levels = {1: nodes}
    for h in range(1, LEVELS - 2):
        if h in SOURCE:
            pairs = [
                (jnp.concatenate(nodes[bit::2], axis=0), weights_ref[CLIMB[h, bit]])
                for bit in range(2)
            ]
        else:
            pairs = [(jnp.concatenate(nodes, axis=0), weights_ref[CLIMB[h, 0]])]
        nodes = as_nodes(split_lanes(multiply(pairs)))
        levels[h + 1] = nodes
    down = None
    for h in range(LEVELS - 2, 0, -1):
        if down is None:
            down = [jnp.zeros((32, LANES), F32)] * 2 ** len(above(TARGET, h))
        else:
            value = split_lanes(jnp.concatenate(down, axis=0))
            parts = [
                as_nodes(multiply([(value, weights_ref[DOWN[h, bit]])]))
                for bit in range(2 if h in TARGET else 1)
            ]
            down = [part for group in zip(*parts) for part in group]
        terms = {}
        for step in (1, 2, 3):
            pair = levels[h][flipped(SOURCE, h, step)], weights_ref[FAR[h, step]]
            terms.setdefault(flipped(TARGET, h, step), []).append(pair)
        for turned, pairs in terms.items():
            down[turned] = down[turned] + multiply(pairs)
    for relative, part in enumerate(down):
        downs[relative] = fold(part)
    for member, node in enumerate(GROUP_Y):
        out_ref[member] = downs[own_target ^ node]
    tie_ref[...] = jnp.zeros_like(tie_ref)


def sum_kernel(parts_ref, tie_ref, out_ref):
    total = parts_ref[0]
    for source in range(1, parts_ref.shape[0]):
        total = total + parts_ref[source]
    out_ref[...] = total


def near_kernel(
    listed_ref,
    own_ref,
    x_ref,
    y_ref,
    xy_ref,
    weights_ref,
    tie_ref,
    out_ref,
    far_ref,
    values,
    rows,
    columns,
    sums,
):
    _, index_y, core = device_index()
    far_ref[...] = multiply(
        [
            (split_lanes(unfold(sent_coeff(ref))), weights_ref[FAR[0, step]])
            for step, ref in enumerate((x_ref, y_ref, xy_ref), 1)
        ]
    )
    low = low_lanes(8)
    for tile in range(LEAVES // 2):
        cols = slice(tile * LANES, tile * LANES + LANES)
        for axis in range(3):
            spread = jnp.broadcast_to(own_ref[64 + axis : 65 + axis, cols], (LANES, LANES))
            columns[axis, cols, :] = spread.T
    for block, ref in enumerate((own_ref, x_ref, y_ref, xy_ref)):
        for tile in range(LEAVES // 2):
            cols = slice(tile * LANES, tile * LANES + LANES)
            first = block * LEAVES + tile * 2
            values[first : first + 2] = split_rows(ref[:64, cols]).T.reshape(2, LEAF, LANES)
            point = ref[64:72, cols]
            rolled = pltpu.roll(point, HALF, 1)
            rows[first] = jnp.where(low, point, rolled)
            rows[first + 1] = jnp.where(low, rolled, point)

    def local(leaf, place):
        listed = listed_ref[leaf, place]
        owner = listed >> 4
        flip_x = (owner >> BITS_Y ^ core) & 1
        flip_y = (owner ^ index_y) & 1
        return (flip_x + 2 * flip_y) * LEAVES + (listed & LEAVES - 1)

    def one_leaf(leaf, carry):
        here = pl.ds(pl.multiple_of(leaf * LEAF, LEAF), LEAF)
        total = None
        for quad in range(3):
            ids = [local(leaf, quad * 4 + place) for place in range(4)]
            kernels = []
            for pair in range(2):
                source = jnp.where(low, rows[ids[pair * 2]], rows[ids[pair * 2 + 1]])
                square = None
                for axis in range(3):
                    delta = columns[axis, here, :] - source[axis : axis + 1]
                    square = delta * delta if square is None else square + delta * delta
                square = jnp.maximum(square, 1e-30)
                distance = square * lax.rsqrt(square)
                scale = ROOT_THREE / LENGTH_SCALE
                decay = jnp.exp2(distance * (-scale * LOG2_E))
                kernel = (distance * (AMPLITUDE * scale) + AMPLITUDE) * decay
                kernels.append(kernel.astype(BF16))
            weight = jnp.concatenate(kernels, axis=1)
            source_values = jnp.concatenate([values[n] for n in ids], axis=0)
            part = jnp.dot(weight, source_values, preferred_element_type=F32)
            total = part if total is None else total + part
        sums[here, :] = total
        return carry

    lax.fori_loop(0, LEAVES, one_leaf, 0, unroll=4)
    for tile in range(LEAVES // 2):
        cols = slice(tile * LANES, tile * LANES + LANES)
        flipped = sums[cols, :].T
        out_ref[:, cols] = flipped[:64] + flipped[64:] + NUGGET * own_ref[:64, cols]


def final_kernel(own_ref, other_ref, far_ref, weights_ref, near_ref, basis_ref, transfer_ref, out_ref):
    first = jnp.full((32, LANES), lax.axis_index("gx") & 1, jnp.int32) == 0
    own = unfold(own_ref[...])
    other = unfold(other_ref[...])
    above = jnp.concatenate([jnp.where(first, own, other), jnp.where(first, other, own)], axis=0)
    down = far_ref[...] + multiply([(split_lanes(above), weights_ref[DOWN[0, 0]])])
    down = down[:, :HALF].astype(BF16)
    for block in range(4):
        cols = slice(block * 256, block * 256 + 256)
        leaf_down = jnp.dot(down, transfer_ref[:, cols], preferred_element_type=F32).astype(BF16)
        far = jnp.dot(leaf_down, block_diagonal(basis_ref[:, cols]), preferred_element_type=F32)
        out_ref[:, cols] = near_ref[:, cols] + far


def call(kernel, out_shape, in_specs, scratch_shapes, *operands, limit=40, cost=None):
    shapes = tuple(jax.ShapeDtypeStruct(shape, dtype) for shape, dtype in out_shape)
    return pl.pallas_call(
        kernel,
        out_shape=shapes,
        in_specs=in_specs,
        out_specs=(VMEM,) * len(shapes),
        scratch_shapes=scratch_shapes,
        cost_estimate=cost,
        compiler_params=pltpu.CompilerParams(vmem_limit_bytes=limit * 1024 * 1024),
    )(*operands)


def exchange(value, name, group):
    return lax.all_to_all(
        value, name, split_axis=0, concat_axis=0, axis_index_groups=[group], tiled=True
    )


def body(
    right_sides,
    points,
    leaf_basis,
    leaf_transfer,
    upper_transfer,
    coupling,
    near_leaves,
    admissible,
):
    width = right_sides.shape[1]
    lifted, send = call(
        up_kernel,
        [((2 ** len(SOURCE) * 2, 16, LANES), F32), ((72, width), F32)],
        [pl.BlockSpec(memory_space=pltpu.HBM)] * 5,
        [
            pltpu.VMEM((3, width), F32),
            pltpu.VMEM((64, width), BF16),
            pltpu.VMEM((64, width), BF16),
            pltpu.VMEM((64, 64), F32),
            pltpu.SemaphoreType.DMA((5,)),
        ],
        right_sides,
        points,
        leaf_basis,
        leaf_transfer,
        upper_transfer,
        limit=60,
    )
    swap = [(i, i ^ 1) for i in range(2**BITS_X)]
    from_x = lax.ppermute(send, "gx", swap)
    from_y = lax.ppermute(send, "gy", [(j, j ^ 1) for j in range(2**BITS_Y)])
    gathered = exchange(lifted, "gx", GROUP_X)
    (weights,) = call(
        weights_kernel,
        [((WEIGHTS, 128, LANES), BF16)],
        [VMEM] * 2 + [SMEM],
        [],
        upper_transfer,
        coupling,
        admissible.T,
    )
    partial, tie = call(
        tree_kernel,
        [((2 ** len(TARGET), 16, LANES), F32), ((8, LANES), F32)],
        [VMEM] * 2,
        [pltpu.VMEM((2 ** len(TARGET), 16, LANES), F32)],
        gathered,
        weights,
        cost=pl.CostEstimate(flops=4 * 10**9, bytes_accessed=12 * 10**6, transcendentals=0),
    )
    parts = exchange(partial, "gy", GROUP_Y)
    from_xy = lax.ppermute(from_y, "gx", swap)
    near, far = call(
        near_kernel,
        [((64, width), F32), ((64, LANES), F32)],
        [SMEM] + [VMEM] * 6,
        [
            pltpu.VMEM((4 * LEAVES, LEAF, LANES), BF16),
            pltpu.VMEM((4 * LEAVES, 8, LANES), F32),
            pltpu.VMEM((3, width, LANES), F32),
            pltpu.VMEM((width, LANES), F32),
        ],
        near_leaves,
        send,
        from_x,
        from_y,
        from_xy,
        weights,
        tie,
    )
    (own,) = call(sum_kernel, [((16, LANES), F32)], [VMEM, ANYWHERE], [], parts, far)
    other = lax.ppermute(own, "gx", swap)
    (product,) = call(
        final_kernel,
        [((64, width), F32)],
        [VMEM] * 7,
        [],
        own,
        other,
        far,
        weights,
        near,
        leaf_basis,
        leaf_transfer,
    )
    return product


def solution(mesh):
    split = P(None, ("gx", "gy"))
    in_specs = (split, split, split, split, P(), P(), P(("gx", "gy"), None), P())
    return jax.shard_map(body, mesh=mesh, in_specs=in_specs, out_specs=split, check_vma=False)
```

profile of v0, /device:TPU:1, one launch (start us, length us, event | category | flops | bytes accessed | tf_op | source)
XLA Modules:
  0.0 50.1 jit_solution(12881068812124680633)
XLA Ops:
  0.0 0.0 copy-start
  0.0 0.0 copy-start.1
  0.0 2.4 %shard_map.82 = (f32[16,16,128]{2,1,0:T(8,128)}, f32[72,1024]{1,0:T(8,128)}) custom-call(f32[64,1024]{1,0:T(8,128)} %right_ref.1, f32[3,1024]{1,0:T(4,128)} %points_ref.1, bf16[64,1024]{1,0:T(8,128)(2,1)} %basis_ref.3, bf16[64,1024]{1,0:T(8,128)(2,1)} %transfer_ref.3, f32[7,2,64,64]{3,2,1,0:T(8,128)} %upper_ref.3), custom_call_target="tpu_custom_call" | custom-call | tf_op jit(solution)/shard_map/pallas_call | solution.py:367
  2.5 13.0 %all-to-all-start = ((f32[16,16,128]{2,1,0:T(8,128)}), f32[16,16,128]{2,1,0:T(8,128)S(1)}, u32[]{:S(2)}, u32[]{:S(2)}) async-start(f32[16,16,128]{2,1,0:T(8,128)} %get-tuple-element.11), calls=%async_computation | async-start | bytes 262144 | tf_op jit(solution)/shard_map/all_to_all | solution.py:379
  15.4 3.2 %collective-permute-start.1 = (f32[72,1024]{1,0:T(8,128)}, f32[72,1024]{1,0:T(8,128)S(1)}, u32[]{:S(2)}, u32[]{:S(2)}) collective-permute-start(f32[72,1024]{1,0:T(8,128)} %get-tuple-element.13.own_ref), channel_id=1, source_target_pairs={{0,1},{1,0},{2,3},{3,2},{4,5},{5,4},{6,7},{7,6},{8,9},{9,8},{10,11... | collective-permute-start | bytes 884744 | tf_op jit(solution)/shard_map/ppermute | solution.py:415
  18.6 0.0 copy-done
  18.7 0.0 copy-done.1
  18.7 0.0 copy-start.5
  18.7 0.7 %copy-done.5 = s32[1020,3]{0,1:T(4,128)S(1)} copy-done((s32[1020,3]{0,1:T(4,128)S(1)}, s32[1020,3]{0,1:T(4,128)}, u32[]{:S(2)}) %copy-start.5) | copy-done | bytes 12264
  19.4 1.7 %shard_map.83.weights_ref = bf16[43,128,128]{2,1,0:T(8,128)(2,1)S(1)} custom-call(f32[7,2,64,64]{3,2,1,0:T(8,128)S(1)} %copy-done, f32[8,3,64,64]{3,2,1,0:T(8,128)S(1)} %copy-done.1, s32[3,1020]{1,0:T(4,128)S(1)} %bitcast.1), custom_call_target="tpu_custom_call" | custom-call | tf_op jit(solution)/shard_map/pallas_call | solution.py:367
  21.1 0.0 copy-start.4
  21.1 0.0 copy-start.6
  21.1 0.5 all-to-all-done.gathered_ref
  21.6 2.9 %shard_map.84 = (f32[32,16,128]{2,1,0:T(8,128)}, f32[8,128]{1,0:T(8,128)S(1)}) custom-call(f32[16,16,128]{2,1,0:T(8,128)S(1)} %all-to-all-done.gathered_ref, bf16[43,128,128]{2,1,0:T(8,128)(2,1)S(1)} %shard_map.83.weights_ref), custom_call_target="tpu_custom_call" | custom-call | flops 4000000000 | bytes 12000000 | tf_op jit(solution)/shard_map/pallas_call | solution.py:367
  24.5 10.2 %all-to-all-start.1 = ((f32[32,16,128]{2,1,0:T(8,128)}), f32[32,16,128]{2,1,0:T(8,128)S(1)}, u32[]{:S(2)}, u32[]{:S(2)}) async-start(f32[32,16,128]{2,1,0:T(8,128)} %get-tuple-element.12), calls=%async_computation.1 | async-start | bytes 524288 | tf_op jit(solution)/shard_map/all_to_all | solution.py:379
  34.7 0.0 copy-done.4
  34.7 2.5 %collective-permute-start = (f32[72,1024]{1,0:T(8,128)S(1)}, f32[72,1024]{1,0:T(8,128)S(1)}, u32[]{:S(2)}, u32[]{:S(2)}) collective-permute-start(f32[72,1024]{1,0:T(8,128)S(1)} %copy-done.4), channel_id=1, source_target_pairs={{0,32},{32,0},{64,96},{96,64},{128,160},{160,128},{192,224},{224,1... | collective-permute-start | bytes 884744 | tf_op jit(solution)/shard_map/ppermute | solution.py:414
  37.2 0.0 collective-permute-done.1.y_ref
  37.2 1.9 %collective-permute-start.2 = (f32[72,1024]{1,0:T(8,128)S(1)}, f32[72,1024]{1,0:T(8,128)S(1)}, u32[]{:S(2)}, u32[]{:S(2)}) collective-permute-start(f32[72,1024]{1,0:T(8,128)S(1)} %collective-permute-done.1.y_ref), channel_id=1, source_target_pairs={{0,32},{32,0},{64,96},{96,64},{128,160},{160,128},{192,224},{224,1... | collective-permute-start | bytes 884744 | tf_op jit(solution)/shard_map/ppermute | solution.py:436
  39.2 0.0 collective-permute-done.x_ref
  39.2 1.5 %collective-permute-done.2.xy_ref = f32[72,1024]{1,0:T(8,128)S(1)} collective-permute-done((f32[72,1024]{1,0:T(8,128)S(1)}, f32[72,1024]{1,0:T(8,128)S(1)}, u32[]{:S(2)}, u32[]{:S(2)}) %collective-permute-start.2) | collective-permute-done | bytes 294944 | tf_op jit(solution)/shard_map/ppermute | solution.py:436
  40.7 0.0 copy-done.6
  40.7 0.0 copy-start.2
  40.7 0.0 copy-start.3
  40.7 4.1 %shard_map.85 = (f32[64,1024]{1,0:T(8,128)S(1)}, f32[64,128]{1,0:T(8,128)S(1)}) custom-call(s32[16,12]{1,0:T(8,128)S(1)} %copy-done.6, f32[72,1024]{1,0:T(8,128)S(1)} %copy-done.4, f32[72,1024]{1,0:T(8,128)S(1)} %collective-permute-done.x_ref, f32[72,1024]{1,0:T(8,128)S(1)} %collective-permute-done.1.y_ref, f32[72,1024]{1,0:T(8,128)S(1)} %collective-permute-done.2.xy_ref, ...), custom_call_target="tpu_custom_call" | custom-call | tf_op jit(solution)/shard_map/pallas_call | solution.py:367
  44.8 0.2 all-to-all-done.1.parts_ref
  45.1 2.9 %collective-permute-start.3 = (f32[16,128]{1,0:T(8,128)S(1)}, f32[16,128]{1,0:T(8,128)S(1)}, u32[]{:S(2)}, u32[]{:S(2)}) collective-permute-start(f32[16,128]{1,0:T(8,128)S(1)} %shard_map.86.own_ref), channel_id=1, source_target_pairs={{0,32},{32,0},{64,96},{96,64},{128,160},{160,128},{192,224},{224,1... | collective-permute-start | bytes 24584 | tf_op jit(solution)/shard_map/ppermute | solution.py:456
  48.0 0.8 %collective-permute-done.3.other_ref = f32[16,128]{1,0:T(8,128)S(1)} collective-permute-done((f32[16,128]{1,0:T(8,128)S(1)}, f32[16,128]{1,0:T(8,128)S(1)}, u32[]{:S(2)}, u32[]{:S(2)}) %collective-permute-start.3) | collective-permute-done | bytes 8224 | tf_op jit(solution)/shard_map/ppermute | solution.py:456
  48.8 0.0 copy-done.2
  48.8 0.0 copy-done.3
  48.8 1.3 %shard_map.87 = f32[64,1024]{1,0:T(8,128)} custom-call(f32[16,128]{1,0:T(8,128)S(1)} %shard_map.86.own_ref, f32[16,128]{1,0:T(8,128)S(1)} %collective-permute-done.3.other_ref, f32[64,128]{1,0:T(8,128)S(1)} %get-tuple-element.15.tie_ref.far_ref, bf16[43,128,128]{2,1,0:T(8,128)(2,1)S(1)} %shard_map.83.weights_ref, f32[64,1024]{1,0:T(8,128)S(1)} %get-tuple-element.16.near_ref, ...), custom_call_target="tpu_custom_call" | custom-call | tf_op jit(solution)/shard_map/pallas_call | solution.py:367
  (1 shorter events, 0.0 us)
Async XLA Ops:
  0.0 18.6 %copy-start = (f32[7,2,64,64]{3,2,1,0:T(8,128)S(1)}, f32[7,2,64,64]{3,2,1,0:T(8,128)}, u32[]{:S(2)}) copy-start(f32[7,2,64,64]{3,2,1,0:T(8,128)} %upper_ref.3) | copy-start | bytes 688132
  0.0 18.7 %copy-start.1 = (f32[8,3,64,64]{3,2,1,0:T(8,128)S(1)}, f32[8,3,64,64]{3,2,1,0:T(8,128)}, u32[]{:S(2)}) copy-start(f32[8,3,64,64]{3,2,1,0:T(8,128)} %coupling_ref.1) | copy-start | bytes 1179652
  2.5 19.2 %all-to-all-start = ((f32[16,16,128]{2,1,0:T(8,128)}), f32[16,16,128]{2,1,0:T(8,128)S(1)}, u32[]{:S(2)}, u32[]{:S(2)}) async-start(f32[16,16,128]{2,1,0:T(8,128)} %get-tuple-element.11), calls=%async_computation | async-start | bytes 262144 | tf_op jit(solution)/shard_map/all_to_all | solution.py:379
  15.4 21.8 %collective-permute-start.1 = (f32[72,1024]{1,0:T(8,128)}, f32[72,1024]{1,0:T(8,128)S(1)}, u32[]{:S(2)}, u32[]{:S(2)}) collective-permute-start(f32[72,1024]{1,0:T(8,128)} %get-tuple-element.13.own_ref), channel_id=1, source_target_pairs={{0,1},{1,0},{2,3},{3,2},{4,5},{5,4},{6,7},{7,6},{8,9},{9,8},{10,11... | collective-permute-start | bytes 884744 | tf_op jit(solution)/shard_map/ppermute | solution.py:415
  18.7 0.7 %copy-start.5 = (s32[1020,3]{0,1:T(4,128)S(1)}, s32[1020,3]{0,1:T(4,128)}, u32[]{:S(2)}) copy-start(s32[1020,3]{0,1:T(4,128)} %param.15) | copy-start | bytes 36724
  21.1 13.6 %copy-start.4 = (f32[72,1024]{1,0:T(8,128)S(1)}, f32[72,1024]{1,0:T(8,128)}, u32[]{:S(2)}) copy-start(f32[72,1024]{1,0:T(8,128)} %get-tuple-element.13.own_ref) | copy-start | bytes 884740
  21.1 19.6 %copy-start.6 = (s32[16,12]{1,0:T(8,128)S(1)}, s32[16,12]{1,0:T(8,128)}, u32[]{:S(2)}) copy-start(s32[16,12]{1,0:T(8,128)} %listed_ref.1) | copy-start | bytes 2308
  24.5 20.5 %all-to-all-start.1 = ((f32[32,16,128]{2,1,0:T(8,128)}), f32[32,16,128]{2,1,0:T(8,128)S(1)}, u32[]{:S(2)}, u32[]{:S(2)}) async-start(f32[32,16,128]{2,1,0:T(8,128)} %get-tuple-element.12), calls=%async_computation.1 | async-start | bytes 524288 | tf_op jit(solution)/shard_map/all_to_all | solution.py:379
  34.7 4.5 %collective-permute-start = (f32[72,1024]{1,0:T(8,128)S(1)}, f32[72,1024]{1,0:T(8,128)S(1)}, u32[]{:S(2)}, u32[]{:S(2)}) collective-permute-start(f32[72,1024]{1,0:T(8,128)S(1)} %copy-done.4), channel_id=1, source_target_pairs={{0,32},{32,0},{64,96},{96,64},{128,160},{160,128},{192,224},{224,1... | collective-permute-start | bytes 884744 | tf_op jit(solution)/shard_map/ppermute | solution.py:414
  37.2 3.5 %collective-permute-start.2 = (f32[72,1024]{1,0:T(8,128)S(1)}, f32[72,1024]{1,0:T(8,128)S(1)}, u32[]{:S(2)}, u32[]{:S(2)}) collective-permute-start(f32[72,1024]{1,0:T(8,128)S(1)} %collective-permute-done.1.y_ref), channel_id=1, source_target_pairs={{0,32},{32,0},{64,96},{96,64},{128,160},{160,128},{192,224},{224,1... | collective-permute-start | bytes 884744 | tf_op jit(solution)/shard_map/ppermute | solution.py:436
  40.7 8.1 %copy-start.2 = (bf16[64,1024]{1,0:T(8,128)(2,1)S(1)}, bf16[64,1024]{1,0:T(8,128)(2,1)}, u32[]{:S(2)}) copy-start(bf16[64,1024]{1,0:T(8,128)(2,1)} %basis_ref.3) | copy-start | bytes 393220
  40.7 8.1 %copy-start.3 = (bf16[64,1024]{1,0:T(8,128)(2,1)S(1)}, bf16[64,1024]{1,0:T(8,128)(2,1)}, u32[]{:S(2)}) copy-start(bf16[64,1024]{1,0:T(8,128)(2,1)} %transfer_ref.3) | copy-start | bytes 393220
  45.1 3.7 %collective-permute-start.3 = (f32[16,128]{1,0:T(8,128)S(1)}, f32[16,128]{1,0:T(8,128)S(1)}, u32[]{:S(2)}, u32[]{:S(2)}) collective-permute-start(f32[16,128]{1,0:T(8,128)S(1)} %shard_map.86.own_ref), channel_id=1, source_target_pairs={{0,32},{32,0},{64,96},{96,64},{128,160},{160,128},{192,224},{224,1... | collective-permute-start | bytes 24584 | tf_op jit(solution)/shard_map/ppermute | solution.py:456
where the time goes:
time: 50.6 us; the launch traced here: 50.1 us
  starting transfers between devices  33.7 us (67%)
  Pallas kernels  12.5 us (25%)
  waiting for transfers between devices  3.04 us (6%)
  local copies, waits for them, and re-layouts  0.74 us (1%)
    all_to_all x2, starting transfers between devices, exchange(): lax.all_to_all(value, name, split_axis=0, concat_axis=0, axis_index_group...  23.2 us
    pallas_call x6, Pallas kernels, call(): pl.pallas_call(kernel, out_shape=shapes, in_specs=in_specs, out_specs=(VM...  12.5 us
    ppermute x1, starting transfers between devices, body(): from_y = lax.ppermute(send, 'gy', [(j, j ^ 1) for j in range(2 ** BITS_Y)])  3.19 us
    ppermute x1, starting transfers between devices, body(): other = lax.ppermute(own, 'gx', swap)  2.9 us
    ppermute x1, starting transfers between devices, body(): from_x = lax.ppermute(send, 'gx', swap)  2.51 us
    ppermute x1, starting transfers between devices, body(): from_xy = lax.ppermute(from_y, 'gx', swap)  1.92 us
    ppermute x1, waiting for transfers between devices, body(): from_xy = lax.ppermute(from_y, 'gx', swap)  1.54 us
  transfers between devices with their start and end apart: 6, of which 4 were waited for; matrix products, arithmetic and copies ran while one was open for 0% of the time, Pallas kernels for 17%

commit v1 on v0

--- a/solution.py
+++ b/solution.py
@@ -1,3 +1,5 @@
+import itertools
+
 import jax
 import jax.numpy as jnp
 from jax import lax
@@ -43,17 +45,20 @@
 GROUP_X = [z * 2 + core for z in (7, 3, 6, 2, 5, 1, 4, 0) for core in (1, 0)]
 GROUP_Y = [x * 8 + y for y in (3, 7, 1, 5, 2, 6, 4, 0) for x in (1, 3, 2, 0)]
 
-CLIMB, DOWN, FAR = {}, {}, {}
-for _h in range(1, LEVELS - 2):
-    for _side in range(2 if _h in SOURCE else 1):
-        CLIMB[_h, _side] = len(CLIMB)
-for _h in range(LEVELS - 2):
-    for _side in range(2 if _h in TARGET else 1):
-        DOWN[_h, _side] = len(CLIMB) + len(DOWN)
+CLIMB, DOWN, CLIMB2, DOWN2, FAR = {}, {}, {}, {}, {}
+ODD = (1, 3, 5)
+_slots = itertools.count()
+for _h in ODD:
+    CLIMB[_h, 0] = next(_slots)
+    for _side in range(2):
+        DOWN[_h, _side] = next(_slots)
+        CLIMB2[_h, _side] = next(_slots)
+        DOWN2[_h, _side] = next(_slots)
+DOWN[0, 0] = next(_slots)
 for _h in range(LEVELS - 1):
     for _step in (1, 2, 3):
-        FAR[_h, _step] = len(CLIMB) + len(DOWN) + len(FAR)
-WEIGHTS = len(CLIMB) + len(DOWN) + len(FAR)
+        FAR[_h, _step] = next(_slots)
+WEIGHTS = next(_slots)
 
 
 def above(chosen, h):
@@ -199,13 +204,19 @@
     def transposed(matrix):
         return jnp.concatenate([matrix, matrix], axis=0).T
 
-    for h in range(LEVELS - 2):
+    out_ref[DOWN[0, 0]] = split_rows(transposed(upper_ref[0, sides[0]]))
+    for h in ODD:
+        low = [upper_ref[h, sides[h] ^ side] for side in range(2)]
+        high = [split_rows(plain(upper_ref[h + 1, sides[h + 1] ^ side])) for side in range(2)]
+        own = split_lanes(plain(low[0]))
+        both = [multiply([(own, matrix)]) for matrix in high]
+        turned = multiply([(split_lanes(plain(low[1])), high[0])])
+        out_ref[CLIMB[h, 0]] = split_rows(plain(low[0]))
         for side in range(2):
-            matrix = upper_ref[h, sides[h] ^ side]
-            if (h, side) in CLIMB:
-                out_ref[CLIMB[h, side]] = split_rows(plain(matrix))
-            if (h, side) in DOWN:
-                out_ref[DOWN[h, side]] = split_rows(transposed(matrix))
+            out_ref[DOWN[h, side]] = split_rows(transposed(low[side]))
+            out_ref[CLIMB2[h, side]] = split_rows(both[side])
+        out_ref[DOWN2[h, 0]] = split_rows(transposed(both[0][:, :HALF]))
+        out_ref[DOWN2[h, 1]] = split_rows(transposed(turned[:, :HALF]))
     for h in range(LEVELS - 1):
         first = 2 * DEVICES - 2 * DEVICES // 2**h
         for step in (1, 2, 3):
@@ -230,33 +241,37 @@
         first = (far_z & 3) * 4 + (far_z >> 2) * 2
         nodes.append(split_lanes(unfold(gathered_ref[first] + gathered_ref[first + 1])))
     levels = {1: nodes}
-    for h in range(1, LEVELS - 2):
-        if h in SOURCE:
-            pairs = [
-                (jnp.concatenate(nodes[bit::2], axis=0), weights_ref[CLIMB[h, bit]])
-                for bit in range(2)
-            ]
-        else:
-            pairs = [(jnp.concatenate(nodes, axis=0), weights_ref[CLIMB[h, 0]])]
+    for h in ODD:
+        pairs = [
+            (jnp.concatenate(nodes[bit::2], axis=0), weights_ref[CLIMB2[h, bit]])
+            for bit in range(2)
+        ]
+        single = multiply([(jnp.concatenate(nodes, axis=0), weights_ref[CLIMB[h, 0]])])
+        levels[h + 1] = as_nodes(split_lanes(single))
         nodes = as_nodes(split_lanes(multiply(pairs)))
-        levels[h + 1] = nodes
-    down = None
-    for h in range(LEVELS - 2, 0, -1):
-        if down is None:
-            down = [jnp.zeros((32, LANES), F32)] * 2 ** len(above(TARGET, h))
-        else:
-            value = split_lanes(jnp.concatenate(down, axis=0))
-            parts = [
-                as_nodes(multiply([(value, weights_ref[DOWN[h, bit]])]))
-                for bit in range(2 if h in TARGET else 1)
-            ]
-            down = [part for group in zip(*parts) for part in group]
+        levels[h + 2] = nodes
+
+    def coupled(h):
         terms = {}
         for step in (1, 2, 3):
             pair = levels[h][flipped(SOURCE, h, step)], weights_ref[FAR[h, step]]
             terms.setdefault(flipped(TARGET, h, step), []).append(pair)
-        for turned, pairs in terms.items():
-            down[turned] = down[turned] + multiply(pairs)
+        return {turned: multiply(pairs) for turned, pairs in terms.items()}
+
+    far = coupled(LEVELS - 2)
+    zero = jnp.zeros((32, LANES), F32)
+    down = [far.get(n, zero) for n in range(2 ** len(above(TARGET, LEVELS - 2)))]
+    for h in reversed(ODD):
+        value = split_lanes(jnp.concatenate(down, axis=0))
+        between = coupled(h + 1)
+        extra = split_lanes(jnp.concatenate([between[0], between[1]], axis=0))
+        parts = [as_nodes(multiply([(value, weights_ref[DOWN2[h, bit]])])) for bit in range(2)]
+        down = [part for group in zip(*parts) for part in group]
+        for bit in range(2):
+            for parent, part in enumerate(as_nodes(multiply([(extra, weights_ref[DOWN[h, bit]])]))):
+                down[2 * parent + bit] = down[2 * parent + bit] + part
+        for turned, part in coupled(h).items():
+            down[turned] = down[turned] + part
     for relative, part in enumerate(down):
         downs[relative] = fold(part)
     for member, node in enumerate(GROUP_Y):

time: 50.6 us -> 49.9 us (0.986)
    pallas_call x6, Pallas kernels: 12.5 us -> 12 us  [call(): pl.pallas_call(kernel, out_shape=shapes, in_specs=in_specs, out_specs=(VM...]
  transfers between devices with their start and end apart: 6 -> 6, of which waited for: 4 -> 3; matrix products, arithmetic and copies ran while one was open for 0% -> 0% of each run, Pallas kernels for 17% -> 17%
where the time goes in v1:
time: 49.9 us; the launch traced here: 49.4 us
  starting transfers between devices  33.9 us (68%)
  Pallas kernels  12 us (24%)
  waiting for transfers between devices  2.64 us (5%)
  local copies, waits for them, and re-layouts  0.74 us (1%)
    all_to_all x2, starting transfers between devices, exchange(): lax.all_to_all(value, name, split_axis=0, concat_axis=0, axis_index_group...  23.2 us
    pallas_call x6, Pallas kernels, call(): pl.pallas_call(kernel, out_shape=shapes, in_specs=in_specs, out_specs=(VM...  12 us
    ppermute x1, starting transfers between devices, body(): from_y = lax.ppermute(send, 'gy', [(j, j ^ 1) for j in range(2 ** BITS_Y)])  3.19 us
    ppermute x1, starting transfers between devices, body(): from_x = lax.ppermute(send, 'gx', swap)  2.81 us
    ppermute x1, starting transfers between devices, body(): other = lax.ppermute(own, 'gx', swap)  2.79 us
    ppermute x1, starting transfers between devices, body(): from_xy = lax.ppermute(from_y, 'gx', swap)  1.92 us
    ppermute x1, waiting for transfers between devices, body(): from_xy = lax.ppermute(from_y, 'gx', swap)  1.54 us
  transfers between devices with their start and end apart: 6, of which 3 were waited for; matrix products, arithmetic and copies ran while one was open for 0% of the time, Pallas kernels for 17%

profile of v1, /device:TPU:1, one launch (start us, length us, event | category | flops | bytes accessed | tf_op | source)
XLA Modules:
  0.0 49.4 jit_solution(1629653926303193219)
XLA Ops:
  0.0 0.0 copy-start
  0.0 0.0 copy-start.1
  0.0 2.4 %shard_map.82 = (f32[16,16,128]{2,1,0:T(8,128)}, f32[72,1024]{1,0:T(8,128)}) custom-call(f32[64,1024]{1,0:T(8,128)} %right_ref.1, f32[3,1024]{1,0:T(4,128)} %points_ref.1, bf16[64,1024]{1,0:T(8,128)(2,1)} %basis_ref.3, bf16[64,1024]{1,0:T(8,128)(2,1)} %transfer_ref.3, f32[7,2,64,64]{3,2,1,0:T(8,128)} %upper_ref.3), custom_call_target="tpu_custom_call" | custom-call | tf_op jit(solution)/shard_map/pallas_call | solution.py:382
  2.5 13.0 %all-to-all-start = ((f32[16,16,128]{2,1,0:T(8,128)}), f32[16,16,128]{2,1,0:T(8,128)S(1)}, u32[]{:S(2)}, u32[]{:S(2)}) async-start(f32[16,16,128]{2,1,0:T(8,128)} %get-tuple-element.11), calls=%async_computation | async-start | bytes 262144 | tf_op jit(solution)/shard_map/all_to_all | solution.py:394
  15.4 3.2 %collective-permute-start.1 = (f32[72,1024]{1,0:T(8,128)}, f32[72,1024]{1,0:T(8,128)S(1)}, u32[]{:S(2)}, u32[]{:S(2)}) collective-permute-start(f32[72,1024]{1,0:T(8,128)} %get-tuple-element.13.own_ref), channel_id=1, source_target_pairs={{0,1},{1,0},{2,3},{3,2},{4,5},{5,4},{6,7},{7,6},{8,9},{9,8},{10,11... | collective-permute-start | bytes 884744 | tf_op jit(solution)/shard_map/ppermute | solution.py:430
  18.6 0.0 copy-done
  18.7 0.0 copy-done.1
  18.7 0.0 copy-start.5
  18.7 0.7 %copy-done.5 = s32[1020,3]{0,1:T(4,128)S(1)} copy-done((s32[1020,3]{0,1:T(4,128)S(1)}, s32[1020,3]{0,1:T(4,128)}, u32[]{:S(2)}) %copy-start.5) | copy-done | bytes 12264
  19.4 1.9 %shard_map.83.weights_ref = bf16[46,128,128]{2,1,0:T(8,128)(2,1)S(1)} custom-call(f32[7,2,64,64]{3,2,1,0:T(8,128)S(1)} %copy-done, f32[8,3,64,64]{3,2,1,0:T(8,128)S(1)} %copy-done.1, s32[3,1020]{1,0:T(4,128)S(1)} %bitcast.1), custom_call_target="tpu_custom_call" | custom-call | tf_op jit(solution)/shard_map/pallas_call | solution.py:382
  21.3 0.0 copy-start.4
  21.3 0.0 copy-start.6
  21.3 0.3 all-to-all-done.gathered_ref
  21.6 2.2 %shard_map.84 = (f32[32,16,128]{2,1,0:T(8,128)}, f32[8,128]{1,0:T(8,128)S(1)}) custom-call(f32[16,16,128]{2,1,0:T(8,128)S(1)} %all-to-all-done.gathered_ref, bf16[46,128,128]{2,1,0:T(8,128)(2,1)S(1)} %shard_map.83.weights_ref), custom_call_target="tpu_custom_call" | custom-call | flops 4000000000 | bytes 12000000 | tf_op jit(solution)/shard_map/pallas_call | solution.py:382
  23.8 10.2 %all-to-all-start.1 = ((f32[32,16,128]{2,1,0:T(8,128)}), f32[32,16,128]{2,1,0:T(8,128)S(1)}, u32[]{:S(2)}, u32[]{:S(2)}) async-start(f32[32,16,128]{2,1,0:T(8,128)} %get-tuple-element.12), calls=%async_computation.1 | async-start | bytes 524288 | tf_op jit(solution)/shard_map/all_to_all | solution.py:394
  34.0 0.0 copy-done.4
  34.0 0.0 copy-start.2
  34.0 0.0 copy-start.3
  34.0 2.8 %collective-permute-start = (f32[72,1024]{1,0:T(8,128)S(1)}, f32[72,1024]{1,0:T(8,128)S(1)}, u32[]{:S(2)}, u32[]{:S(2)}) collective-permute-start(f32[72,1024]{1,0:T(8,128)S(1)} %copy-done.4), channel_id=1, source_target_pairs={{0,32},{32,0},{64,96},{96,64},{128,160},{160,128},{192,224},{224,1... | collective-permute-start | bytes 884744 | tf_op jit(solution)/shard_map/ppermute | solution.py:429
  36.9 0.0 collective-permute-done.1.y_ref
  36.9 1.9 %collective-permute-start.2 = (f32[72,1024]{1,0:T(8,128)S(1)}, f32[72,1024]{1,0:T(8,128)S(1)}, u32[]{:S(2)}, u32[]{:S(2)}) collective-permute-start(f32[72,1024]{1,0:T(8,128)S(1)} %collective-permute-done.1.y_ref), channel_id=1, source_target_pairs={{0,32},{32,0},{64,96},{96,64},{128,160},{160,128},{192,224},{224,1... | collective-permute-start | bytes 884744 | tf_op jit(solution)/shard_map/ppermute | solution.py:451
  38.8 0.0 collective-permute-done.x_ref
  38.8 1.5 %collective-permute-done.2.xy_ref = f32[72,1024]{1,0:T(8,128)S(1)} collective-permute-done((f32[72,1024]{1,0:T(8,128)S(1)}, f32[72,1024]{1,0:T(8,128)S(1)}, u32[]{:S(2)}, u32[]{:S(2)}) %collective-permute-start.2) | collective-permute-done | bytes 294944 | tf_op jit(solution)/shard_map/ppermute | solution.py:451
  40.3 0.0 copy-done.6
  40.3 4.1 %shard_map.85 = (f32[64,1024]{1,0:T(8,128)S(1)}, f32[64,128]{1,0:T(8,128)S(1)}) custom-call(s32[16,12]{1,0:T(8,128)S(1)} %copy-done.6, f32[72,1024]{1,0:T(8,128)S(1)} %copy-done.4, f32[72,1024]{1,0:T(8,128)S(1)} %collective-permute-done.x_ref, f32[72,1024]{1,0:T(8,128)S(1)} %collective-permute-done.1.y_ref, f32[72,1024]{1,0:T(8,128)S(1)} %collective-permute-done.2.xy_ref, ...), custom_call_target="tpu_custom_call" | custom-call | tf_op jit(solution)/shard_map/pallas_call | solution.py:382
  44.4 0.0 all-to-all-done.1.parts_ref
  44.5 2.8 %collective-permute-start.3 = (f32[16,128]{1,0:T(8,128)S(1)}, f32[16,128]{1,0:T(8,128)S(1)}, u32[]{:S(2)}, u32[]{:S(2)}) collective-permute-start(f32[16,128]{1,0:T(8,128)S(1)} %shard_map.86.own_ref), channel_id=1, source_target_pairs={{0,32},{32,0},{64,96},{96,64},{128,160},{160,128},{192,224},{224,1... | collective-permute-start | bytes 24584 | tf_op jit(solution)/shard_map/ppermute | solution.py:471
  47.3 0.8 %collective-permute-done.3.other_ref = f32[16,128]{1,0:T(8,128)S(1)} collective-permute-done((f32[16,128]{1,0:T(8,128)S(1)}, f32[16,128]{1,0:T(8,128)S(1)}, u32[]{:S(2)}, u32[]{:S(2)}) %collective-permute-start.3) | collective-permute-done | bytes 8224 | tf_op jit(solution)/shard_map/ppermute | solution.py:471
  48.1 0.0 copy-done.2
  48.1 0.0 copy-done.3
  48.1 1.3 %shard_map.87 = f32[64,1024]{1,0:T(8,128)} custom-call(f32[16,128]{1,0:T(8,128)S(1)} %shard_map.86.own_ref, f32[16,128]{1,0:T(8,128)S(1)} %collective-permute-done.3.other_ref, f32[64,128]{1,0:T(8,128)S(1)} %get-tuple-element.15.tie_ref.far_ref, bf16[46,128,128]{2,1,0:T(8,128)(2,1)S(1)} %shard_map.83.weights_ref, f32[64,1024]{1,0:T(8,128)S(1)} %get-tuple-element.16.near_ref, ...), custom_call_target="tpu_custom_call" | custom-call | tf_op jit(solution)/shard_map/pallas_call | solution.py:382
  (1 shorter events, 0.0 us)
Async XLA Ops:
  0.0 18.6 %copy-start = (f32[7,2,64,64]{3,2,1,0:T(8,128)S(1)}, f32[7,2,64,64]{3,2,1,0:T(8,128)}, u32[]{:S(2)}) copy-start(f32[7,2,64,64]{3,2,1,0:T(8,128)} %upper_ref.3) | copy-start | bytes 688132
  0.0 18.7 %copy-start.1 = (f32[8,3,64,64]{3,2,1,0:T(8,128)S(1)}, f32[8,3,64,64]{3,2,1,0:T(8,128)}, u32[]{:S(2)}) copy-start(f32[8,3,64,64]{3,2,1,0:T(8,128)} %coupling_ref.1) | copy-start | bytes 1179652
  2.5 19.2 %all-to-all-start = ((f32[16,16,128]{2,1,0:T(8,128)}), f32[16,16,128]{2,1,0:T(8,128)S(1)}, u32[]{:S(2)}, u32[]{:S(2)}) async-start(f32[16,16,128]{2,1,0:T(8,128)} %get-tuple-element.11), calls=%async_computation | async-start | bytes 262144 | tf_op jit(solution)/shard_map/all_to_all | solution.py:394
  15.4 21.4 %collective-permute-start.1 = (f32[72,1024]{1,0:T(8,128)}, f32[72,1024]{1,0:T(8,128)S(1)}, u32[]{:S(2)}, u32[]{:S(2)}) collective-permute-start(f32[72,1024]{1,0:T(8,128)} %get-tuple-element.13.own_ref), channel_id=1, source_target_pairs={{0,1},{1,0},{2,3},{3,2},{4,5},{5,4},{6,7},{7,6},{8,9},{9,8},{10,11... | collective-permute-start | bytes 884744 | tf_op jit(solution)/shard_map/ppermute | solution.py:430
  18.7 0.7 %copy-start.5 = (s32[1020,3]{0,1:T(4,128)S(1)}, s32[1020,3]{0,1:T(4,128)}, u32[]{:S(2)}) copy-start(s32[1020,3]{0,1:T(4,128)} %param.15) | copy-start | bytes 36724
  21.3 12.7 %copy-start.4 = (f32[72,1024]{1,0:T(8,128)S(1)}, f32[72,1024]{1,0:T(8,128)}, u32[]{:S(2)}) copy-start(f32[72,1024]{1,0:T(8,128)} %get-tuple-element.13.own_ref) | copy-start | bytes 884740
  21.3 19.0 %copy-start.6 = (s32[16,12]{1,0:T(8,128)S(1)}, s32[16,12]{1,0:T(8,128)}, u32[]{:S(2)}) copy-start(s32[16,12]{1,0:T(8,128)} %listed_ref.1) | copy-start | bytes 2308
  23.8 20.6 %all-to-all-start.1 = ((f32[32,16,128]{2,1,0:T(8,128)}), f32[32,16,128]{2,1,0:T(8,128)S(1)}, u32[]{:S(2)}, u32[]{:S(2)}) async-start(f32[32,16,128]{2,1,0:T(8,128)} %get-tuple-element.12), calls=%async_computation.1 | async-start | bytes 524288 | tf_op jit(solution)/shard_map/all_to_all | solution.py:394
  34.0 14.1 %copy-start.2 = (bf16[64,1024]{1,0:T(8,128)(2,1)S(1)}, bf16[64,1024]{1,0:T(8,128)(2,1)}, u32[]{:S(2)}) copy-start(bf16[64,1024]{1,0:T(8,128)(2,1)} %basis_ref.3) | copy-start | bytes 393220
  34.0 14.1 %copy-start.3 = (bf16[64,1024]{1,0:T(8,128)(2,1)S(1)}, bf16[64,1024]{1,0:T(8,128)(2,1)}, u32[]{:S(2)}) copy-start(bf16[64,1024]{1,0:T(8,128)(2,1)} %transfer_ref.3) | copy-start | bytes 393220
  34.0 4.8 %collective-permute-start = (f32[72,1024]{1,0:T(8,128)S(1)}, f32[72,1024]{1,0:T(8,128)S(1)}, u32[]{:S(2)}, u32[]{:S(2)}) collective-permute-start(f32[72,1024]{1,0:T(8,128)S(1)} %copy-done.4), channel_id=1, source_target_pairs={{0,32},{32,0},{64,96},{96,64},{128,160},{160,128},{192,224},{224,1... | collective-permute-start | bytes 884744 | tf_op jit(solution)/shard_map/ppermute | solution.py:429
  36.9 3.5 %collective-permute-start.2 = (f32[72,1024]{1,0:T(8,128)S(1)}, f32[72,1024]{1,0:T(8,128)S(1)}, u32[]{:S(2)}, u32[]{:S(2)}) collective-permute-start(f32[72,1024]{1,0:T(8,128)S(1)} %collective-permute-done.1.y_ref), channel_id=1, source_target_pairs={{0,32},{32,0},{64,96},{96,64},{128,160},{160,128},{192,224},{224,1... | collective-permute-start | bytes 884744 | tf_op jit(solution)/shard_map/ppermute | solution.py:451
  44.5 3.6 %collective-permute-start.3 = (f32[16,128]{1,0:T(8,128)S(1)}, f32[16,128]{1,0:T(8,128)S(1)}, u32[]{:S(2)}, u32[]{:S(2)}) collective-permute-start(f32[16,128]{1,0:T(8,128)S(1)} %shard_map.86.own_ref), channel_id=1, source_target_pairs={{0,32},{32,0},{64,96},{96,64},{128,160},{160,128},{192,224},{224,1... | collective-permute-start | bytes 24584 | tf_op jit(solution)/shard_map/ppermute | solution.py:471

commit v2 on v1

--- a/solution.py
+++ b/solution.py
@@ -113,18 +113,25 @@
     ]
     for copy in copies:
         copy.start()
-    for copy in copies:
+    copies[1].wait()
+    diagonals = [block_diagonal(basis_in[:, b * 256 : b * 256 + 256]) for b in range(4)]
+    copies[0].wait()
+    leaf_coeffs = [
+        lax.dot_general(
+            send_ref[:64, b * 256 : b * 256 + 256].astype(BF16),
+            diagonals[b],
+            NT,
+            preferred_element_type=F32,
+        ).astype(BF16)
+        for b in range(4)
+    ]
+    for copy in copies[2:]:
         copy.wait()
     total = None
     for block in range(4):
-        cols = slice(block * 256, block * 256 + 256)
-        rounded = send_ref[:64, cols].astype(BF16)
-        leaf_coeff = lax.dot_general(
-            rounded, block_diagonal(basis_in[:, cols]), NT, preferred_element_type=F32
-        ).astype(BF16)
-        transfer = transfer_in[:, cols]
+        transfer = transfer_in[:, block * 256 : block * 256 + 256]
         part = lax.dot_general(
-            leaf_coeff,
+            leaf_coeffs[block],
             jnp.concatenate([transfer, transfer], axis=0),
             NT,
             preferred_element_type=F32,
@@ -356,7 +363,7 @@
         sums[here, :] = total
         return carry
 
-    lax.fori_loop(0, LEAVES, one_leaf, 0, unroll=4)
+    lax.fori_loop(0, LEAVES, one_leaf, 0, unroll=8)
     for tile in range(LEAVES // 2):
         cols = slice(tile * LANES, tile * LANES + LANES)
         flipped = sums[cols, :].T

time: 49.9 us -> 50 us (level)
  transfers between devices with their start and end apart: 6 -> 6, of which waited for: 3 -> 3; matrix products, arithmetic and copies ran while one was open for 0% -> 0% of each run, Pallas kernels for 17% -> 16%
where the time goes in v2:
time: 50 us; the launch traced here: 49.5 us
  starting transfers between devices  34.1 us (68%)
  Pallas kernels  11.8 us (24%)
  waiting for transfers between devices  2.64 us (5%)
  local copies, waits for them, and re-layouts  0.74 us (1%)
    all_to_all x2, starting transfers between devices, exchange(): lax.all_to_all(value, name, split_axis=0, concat_axis=0, axis_index_group...  23.2 us
    pallas_call x6, Pallas kernels, call(): pl.pallas_call(kernel, out_shape=shapes, in_specs=in_specs, out_specs=(VM...  11.8 us
    ppermute x1, starting transfers between devices, body(): from_y = lax.ppermute(send, 'gy', [(j, j ^ 1) for j in range(2 ** BITS_Y)])  3.19 us
    ppermute x1, starting transfers between devices, body(): other = lax.ppermute(own, 'gx', swap)  3.03 us
    ppermute x1, starting transfers between devices, body(): from_x = lax.ppermute(send, 'gx', swap)  2.81 us
    ppermute x1, starting transfers between devices, body(): from_xy = lax.ppermute(from_y, 'gx', swap)  1.92 us
    ppermute x1, waiting for transfers between devices, body(): from_xy = lax.ppermute(from_y, 'gx', swap)  1.54 us
  transfers between devices with their start and end apart: 6, of which 3 were waited for; matrix products, arithmetic and copies ran while one was open for 0% of the time, Pallas kernels for 16%

profile of v2, /device:TPU:1, one launch (start us, length us, event | category | flops | bytes accessed | tf_op | source)
XLA Modules:
  0.0 49.5 jit_solution(11807321202834782592)
XLA Ops:
  0.0 0.0 copy-start
  0.0 0.0 copy-start.1
  0.0 2.5 %shard_map.82 = (f32[16,16,128]{2,1,0:T(8,128)}, f32[72,1024]{1,0:T(8,128)}) custom-call(f32[64,1024]{1,0:T(8,128)} %right_ref.1, f32[3,1024]{1,0:T(4,128)} %points_ref.1, bf16[64,1024]{1,0:T(8,128)(2,1)} %basis_ref.3, bf16[64,1024]{1,0:T(8,128)(2,1)} %transfer_ref.3, f32[7,2,64,64]{3,2,1,0:T(8,128)} %upper_ref.3), custom_call_target="tpu_custom_call" | custom-call | tf_op jit(solution)/shard_map/pallas_call | solution.py:389
  2.5 13.0 %all-to-all-start = ((f32[16,16,128]{2,1,0:T(8,128)}), f32[16,16,128]{2,1,0:T(8,128)S(1)}, u32[]{:S(2)}, u32[]{:S(2)}) async-start(f32[16,16,128]{2,1,0:T(8,128)} %get-tuple-element.11), calls=%async_computation | async-start | bytes 262144 | tf_op jit(solution)/shard_map/all_to_all | solution.py:401
  15.5 3.2 %collective-permute-start.1 = (f32[72,1024]{1,0:T(8,128)}, f32[72,1024]{1,0:T(8,128)S(1)}, u32[]{:S(2)}, u32[]{:S(2)}) collective-permute-start(f32[72,1024]{1,0:T(8,128)} %get-tuple-element.13.own_ref), channel_id=1, source_target_pairs={{0,1},{1,0},{2,3},{3,2},{4,5},{5,4},{6,7},{7,6},{8,9},{9,8},{10,11... | collective-permute-start | bytes 884744 | tf_op jit(solution)/shard_map/ppermute | solution.py:437
  18.7 0.0 copy-done
  18.7 0.0 copy-done.1
  18.8 0.0 copy-start.5
  18.8 0.7 %copy-done.5 = s32[1020,3]{0,1:T(4,128)S(1)} copy-done((s32[1020,3]{0,1:T(4,128)S(1)}, s32[1020,3]{0,1:T(4,128)}, u32[]{:S(2)}) %copy-start.5) | copy-done | bytes 12264
  19.5 1.9 %shard_map.83.weights_ref = bf16[46,128,128]{2,1,0:T(8,128)(2,1)S(1)} custom-call(f32[7,2,64,64]{3,2,1,0:T(8,128)S(1)} %copy-done, f32[8,3,64,64]{3,2,1,0:T(8,128)S(1)} %copy-done.1, s32[3,1020]{1,0:T(4,128)S(1)} %bitcast.1), custom_call_target="tpu_custom_call" | custom-call | tf_op jit(solution)/shard_map/pallas_call | solution.py:389
  21.4 0.0 copy-start.4
  21.4 0.0 copy-start.6
  21.4 0.3 all-to-all-done.gathered_ref
  21.7 2.2 %shard_map.84 = (f32[32,16,128]{2,1,0:T(8,128)}, f32[8,128]{1,0:T(8,128)S(1)}) custom-call(f32[16,16,128]{2,1,0:T(8,128)S(1)} %all-to-all-done.gathered_ref, bf16[46,128,128]{2,1,0:T(8,128)(2,1)S(1)} %shard_map.83.weights_ref), custom_call_target="tpu_custom_call" | custom-call | flops 4000000000 | bytes 12000000 | tf_op jit(solution)/shard_map/pallas_call | solution.py:389
  23.9 10.2 %all-to-all-start.1 = ((f32[32,16,128]{2,1,0:T(8,128)}), f32[32,16,128]{2,1,0:T(8,128)S(1)}, u32[]{:S(2)}, u32[]{:S(2)}) async-start(f32[32,16,128]{2,1,0:T(8,128)} %get-tuple-element.12), calls=%async_computation.1 | async-start | bytes 524288 | tf_op jit(solution)/shard_map/all_to_all | solution.py:401
  34.1 0.0 copy-done.4
  34.1 0.0 copy-start.2
  34.1 0.0 copy-start.3
  34.1 2.8 %collective-permute-start = (f32[72,1024]{1,0:T(8,128)S(1)}, f32[72,1024]{1,0:T(8,128)S(1)}, u32[]{:S(2)}, u32[]{:S(2)}) collective-permute-start(f32[72,1024]{1,0:T(8,128)S(1)} %copy-done.4), channel_id=1, source_target_pairs={{0,32},{32,0},{64,96},{96,64},{128,160},{160,128},{192,224},{224,1... | collective-permute-start | bytes 884744 | tf_op jit(solution)/shard_map/ppermute | solution.py:436
  36.9 0.0 collective-permute-done.1.y_ref
  36.9 1.9 %collective-permute-start.2 = (f32[72,1024]{1,0:T(8,128)S(1)}, f32[72,1024]{1,0:T(8,128)S(1)}, u32[]{:S(2)}, u32[]{:S(2)}) collective-permute-start(f32[72,1024]{1,0:T(8,128)S(1)} %collective-permute-done.1.y_ref), channel_id=1, source_target_pairs={{0,32},{32,0},{64,96},{96,64},{128,160},{160,128},{192,224},{224,1... | collective-permute-start | bytes 884744 | tf_op jit(solution)/shard_map/ppermute | solution.py:458
  38.9 0.0 collective-permute-done.x_ref
  38.9 1.5 %collective-permute-done.2.xy_ref = f32[72,1024]{1,0:T(8,128)S(1)} collective-permute-done((f32[72,1024]{1,0:T(8,128)S(1)}, f32[72,1024]{1,0:T(8,128)S(1)}, u32[]{:S(2)}, u32[]{:S(2)}) %collective-permute-start.2) | collective-permute-done | bytes 294944 | tf_op jit(solution)/shard_map/ppermute | solution.py:458
  40.4 0.0 copy-done.6
  40.4 3.8 %shard_map.85 = (f32[64,1024]{1,0:T(8,128)S(1)}, f32[64,128]{1,0:T(8,128)S(1)}) custom-call(s32[16,12]{1,0:T(8,128)S(1)} %copy-done.6, f32[72,1024]{1,0:T(8,128)S(1)} %copy-done.4, f32[72,1024]{1,0:T(8,128)S(1)} %collective-permute-done.x_ref, f32[72,1024]{1,0:T(8,128)S(1)} %collective-permute-done.1.y_ref, f32[72,1024]{1,0:T(8,128)S(1)} %collective-permute-done.2.xy_ref, ...), custom_call_target="tpu_custom_call" | custom-call | tf_op jit(solution)/shard_map/pallas_call | solution.py:389
  44.3 0.0 all-to-all-done.1.parts_ref
  44.3 3.0 %collective-permute-start.3 = (f32[16,128]{1,0:T(8,128)S(1)}, f32[16,128]{1,0:T(8,128)S(1)}, u32[]{:S(2)}, u32[]{:S(2)}) collective-permute-start(f32[16,128]{1,0:T(8,128)S(1)} %shard_map.86.own_ref), channel_id=1, source_target_pairs={{0,32},{32,0},{64,96},{96,64},{128,160},{160,128},{192,224},{224,1... | collective-permute-start | bytes 24584 | tf_op jit(solution)/shard_map/ppermute | solution.py:478
  47.4 0.8 %collective-permute-done.3.other_ref = f32[16,128]{1,0:T(8,128)S(1)} collective-permute-done((f32[16,128]{1,0:T(8,128)S(1)}, f32[16,128]{1,0:T(8,128)S(1)}, u32[]{:S(2)}, u32[]{:S(2)}) %collective-permute-start.3) | collective-permute-done | bytes 8224 | tf_op jit(solution)/shard_map/ppermute | solution.py:478
  48.2 0.0 copy-done.2
  48.2 0.0 copy-done.3
  48.2 1.3 %shard_map.87 = f32[64,1024]{1,0:T(8,128)} custom-call(f32[16,128]{1,0:T(8,128)S(1)} %shard_map.86.own_ref, f32[16,128]{1,0:T(8,128)S(1)} %collective-permute-done.3.other_ref, f32[64,128]{1,0:T(8,128)S(1)} %get-tuple-element.15.tie_ref.far_ref, bf16[46,128,128]{2,1,0:T(8,128)(2,1)S(1)} %shard_map.83.weights_ref, f32[64,1024]{1,0:T(8,128)S(1)} %get-tuple-element.16.near_ref, ...), custom_call_target="tpu_custom_call" | custom-call | tf_op jit(solution)/shard_map/pallas_call | solution.py:389
  (1 shorter events, 0.0 us)
Async XLA Ops:
  0.0 18.7 %copy-start = (f32[7,2,64,64]{3,2,1,0:T(8,128)S(1)}, f32[7,2,64,64]{3,2,1,0:T(8,128)}, u32[]{:S(2)}) copy-start(f32[7,2,64,64]{3,2,1,0:T(8,128)} %upper_ref.3) | copy-start | bytes 688132
  0.0 18.7 %copy-start.1 = (f32[8,3,64,64]{3,2,1,0:T(8,128)S(1)}, f32[8,3,64,64]{3,2,1,0:T(8,128)}, u32[]{:S(2)}) copy-start(f32[8,3,64,64]{3,2,1,0:T(8,128)} %coupling_ref.1) | copy-start | bytes 1179652
  2.5 19.2 %all-to-all-start = ((f32[16,16,128]{2,1,0:T(8,128)}), f32[16,16,128]{2,1,0:T(8,128)S(1)}, u32[]{:S(2)}, u32[]{:S(2)}) async-start(f32[16,16,128]{2,1,0:T(8,128)} %get-tuple-element.11), calls=%async_computation | async-start | bytes 262144 | tf_op jit(solution)/shard_map/all_to_all | solution.py:401
  15.5 21.4 %collective-permute-start.1 = (f32[72,1024]{1,0:T(8,128)}, f32[72,1024]{1,0:T(8,128)S(1)}, u32[]{:S(2)}, u32[]{:S(2)}) collective-permute-start(f32[72,1024]{1,0:T(8,128)} %get-tuple-element.13.own_ref), channel_id=1, source_target_pairs={{0,1},{1,0},{2,3},{3,2},{4,5},{5,4},{6,7},{7,6},{8,9},{9,8},{10,11... | collective-permute-start | bytes 884744 | tf_op jit(solution)/shard_map/ppermute | solution.py:437
  18.8 0.7 %copy-start.5 = (s32[1020,3]{0,1:T(4,128)S(1)}, s32[1020,3]{0,1:T(4,128)}, u32[]{:S(2)}) copy-start(s32[1020,3]{0,1:T(4,128)} %param.15) | copy-start | bytes 36724
  21.4 12.7 %copy-start.4 = (f32[72,1024]{1,0:T(8,128)S(1)}, f32[72,1024]{1,0:T(8,128)}, u32[]{:S(2)}) copy-start(f32[72,1024]{1,0:T(8,128)} %get-tuple-element.13.own_ref) | copy-start | bytes 884740
  21.4 19.0 %copy-start.6 = (s32[16,12]{1,0:T(8,128)S(1)}, s32[16,12]{1,0:T(8,128)}, u32[]{:S(2)}) copy-start(s32[16,12]{1,0:T(8,128)} %listed_ref.1) | copy-start | bytes 2308
  23.9 20.4 %all-to-all-start.1 = ((f32[32,16,128]{2,1,0:T(8,128)}), f32[32,16,128]{2,1,0:T(8,128)S(1)}, u32[]{:S(2)}, u32[]{:S(2)}) async-start(f32[32,16,128]{2,1,0:T(8,128)} %get-tuple-element.12), calls=%async_computation.1 | async-start | bytes 524288 | tf_op jit(solution)/shard_map/all_to_all | solution.py:401
  34.1 14.1 %copy-start.2 = (bf16[64,1024]{1,0:T(8,128)(2,1)S(1)}, bf16[64,1024]{1,0:T(8,128)(2,1)}, u32[]{:S(2)}) copy-start(bf16[64,1024]{1,0:T(8,128)(2,1)} %basis_ref.3) | copy-start | bytes 393220
  34.1 14.1 %copy-start.3 = (bf16[64,1024]{1,0:T(8,128)(2,1)S(1)}, bf16[64,1024]{1,0:T(8,128)(2,1)}, u32[]{:S(2)}) copy-start(bf16[64,1024]{1,0:T(8,128)(2,1)} %transfer_ref.3) | copy-start | bytes 393220
  34.1 4.8 %collective-permute-start = (f32[72,1024]{1,0:T(8,128)S(1)}, f32[72,1024]{1,0:T(8,128)S(1)}, u32[]{:S(2)}, u32[]{:S(2)}) collective-permute-start(f32[72,1024]{1,0:T(8,128)S(1)} %copy-done.4), channel_id=1, source_target_pairs={{0,32},{32,0},{64,96},{96,64},{128,160},{160,128},{192,224},{224,1... | collective-permute-start | bytes 884744 | tf_op jit(solution)/shard_map/ppermute | solution.py:436
  36.9 3.5 %collective-permute-start.2 = (f32[72,1024]{1,0:T(8,128)S(1)}, f32[72,1024]{1,0:T(8,128)S(1)}, u32[]{:S(2)}, u32[]{:S(2)}) collective-permute-start(f32[72,1024]{1,0:T(8,128)S(1)} %collective-permute-done.1.y_ref), channel_id=1, source_target_pairs={{0,32},{32,0},{64,96},{96,64},{128,160},{160,128},{192,224},{224,1... | collective-permute-start | bytes 884744 | tf_op jit(solution)/shard_map/ppermute | solution.py:458
  44.3 3.8 %collective-permute-start.3 = (f32[16,128]{1,0:T(8,128)S(1)}, f32[16,128]{1,0:T(8,128)S(1)}, u32[]{:S(2)}, u32[]{:S(2)}) collective-permute-start(f32[16,128]{1,0:T(8,128)S(1)} %shard_map.86.own_ref), channel_id=1, source_target_pairs={{0,32},{32,0},{64,96},{96,64},{128,160},{160,128},{192,224},{224,1... | collective-permute-start | bytes 24584 | tf_op jit(solution)/shard_map/ppermute | solution.py:478
